TPU v7x, 32 devices: a whole 2x2x4 slice. The times are simulated.
32 devices in a mesh: grp: 4 (over y, x), inner: 8 (over z, core).
Axes of the slice: x: 2, y: 2, z: 4, core: 2. Of those that a mesh axis runs over, the one named last changes fastest.
Arguments:
- embeds: bfloat16 [4096, 1024], P(('grp', 'inner')), may hold values from -1.05 to 1.05
- fine_centroids: bfloat16 [8192, 1024], P('inner'), may hold values from -1.05 to 1.05
- coarse_centroids: bfloat16 [512, 1024], replicated, may hold values from -0.39375 to 0.39375
Outputs:
- fine_update: float32 [8192, 1024], P('inner')
- coarse_update: float32 [512, 1024], replicated
All inputs are finite; a program needn't handle non-finite values.
Results may differ from a plain program's by a relative error of at most 0.0044.
Values may be sent and summed in bfloat16 or wider, within the bound.
A program may use at most 64 MiB of HBM per device.

v0:
```python
import jax
import jax.numpy as jnp
from jax import lax
from jax.sharding import PartitionSpec as P

temper = 0.02
shrink = 1.0
anchor = 8.0


def row_scores(row_block, fine_cent, fine_sq):
    inner_prod = lax.dot_general(
        row_block, fine_cent, (((1,), (1,)), ((), ())), preferred_element_type=jnp.float32
    )
    return (inner_prod - 0.5 * fine_sq) / temper


def coarse_softmax(fine_low, coarse_cent, coarse_sq):
    logits = (
        lax.dot_general(
            fine_low, coarse_cent, (((1,), (1,)), ((), ())), preferred_element_type=jnp.float32
        )
        - 0.5 * coarse_sq
    ) / temper
    shifted = jnp.exp(logits - jnp.max(logits, axis=1, keepdims=True))
    return shifted / jnp.sum(shifted, axis=1, keepdims=True)


def prior_of(fine_cent, coarse_cent, coarse_sq):
    parent = coarse_softmax(fine_cent, coarse_cent, coarse_sq).astype(jnp.bfloat16)
    return jnp.dot(parent, coarse_cent, preferred_element_type=jnp.float32)


def update_terms(moment, mass_sum, prior_mean, coarse_cent, coarse_sq):
    weight = mass_sum + shrink
    fine_new = (moment + shrink * prior_mean) / weight[:, None]
    fine_low = fine_new.astype(jnp.bfloat16)
    child_prob = coarse_softmax(fine_low, coarse_cent, coarse_sq)
    share_low = (child_prob * weight[:, None]).astype(jnp.bfloat16)
    numerator = lax.dot_general(
        share_low, fine_low, (((0,), (0,)), ((), ())), preferred_element_type=jnp.float32
    )
    denominator = jnp.sum(share_low, axis=0, dtype=jnp.float32)
    return (fine_new, numerator, denominator)


def on_device(embeds, fine_centroids, coarse_centroids):
    fine_sq = jnp.sum(jnp.square(fine_centroids.astype(jnp.float32)), axis=1)
    coarse_sq = jnp.sum(jnp.square(coarse_centroids.astype(jnp.float32)), axis=1)
    scores = row_scores(
        lax.all_gather(embeds, "inner", axis=0, tiled=True), fine_centroids, fine_sq
    )
    row_peaks = lax.pmax(jnp.max(scores, axis=1), "inner")
    totals = lax.psum(jnp.sum(jnp.exp(scores - row_peaks[:, None]), axis=1), "inner")
    resp_low = (jnp.exp(scores - row_peaks[:, None]) / totals[:, None]).astype(jnp.bfloat16)
    mass_local = jnp.sum(resp_low, axis=0, dtype=jnp.float32)
    moment_local = lax.dot_general(
        resp_low,
        lax.all_gather(embeds, "inner", axis=0, tiled=True),
        (((0,), (0,)), ((), ())),
        preferred_element_type=jnp.float32,
    )
    prior_mean = prior_of(fine_centroids, coarse_centroids, coarse_sq)
    moment, mass_sum = lax.psum((moment_local, mass_local), "grp")
    fine_update, numerator, denominator = update_terms(
        moment, mass_sum, prior_mean, coarse_centroids, coarse_sq
    )
    numerator, denominator = lax.psum((numerator, denominator), "inner")
    coarse_update = (numerator + anchor * coarse_centroids.astype(jnp.float32)) / (
        denominator[:, None] + anchor
    )
    return (fine_update, coarse_update)


def solution(mesh):
    return jax.shard_map(
        on_device,
        mesh=mesh,
        in_specs=(P(("grp", "inner"), None), P("inner", None), P()),
        out_specs=(P("inner", None), P()),
        check_vma=False,
    )
```

profile of v0, /device:TPU:1, one launch (start us, length us, event | category | flops | bytes accessed | tf_op | source)
XLA Modules:
  0.0 271.8 jit_solution(2665220743582025421)
XLA Ops:
  7.2 0.0 copy-start.1
  7.2 0.0 all-gather.2.cloned.1.call-start
  7.2 0.7 all-gather.2.cloned.1.call-update
  7.9 0.0 all-reduce.3.cloned.1.call-start
  8.0 2.1 multiply_reduce_fusion
  10.0 31.2 %all-gather.2.cloned.1.call-done = bf16[1024,1024]{1,0:T(8,128)(2,1)} async-done(((bf16[128,1024]{1,0:T(8,128)(2,1)}), bf16[1024,1024]{1,0:T(8,128)(2,1)}) %all-gather.2.cloned.1.call-update) | async-done | bytes 2097168 | tf_op jit(solution)/shard_map/all_gather | solution.py:51
  41.2 0.0 copy-done.1
  41.2 6.0 %fusion = (f32[1024]{0:T(1024)S(1)}, f32[1024,1024]{0,1:T(8,128)}) fusion(f32[1024]{0:T(1024)S(1)} %broadcast_multiply_fusion, bf16[1024,1024]{1,0:T(8,128)(2,1)} %all-gather.2.cloned.1.call-done, bf16[1024,1024]{1,0:T(8,128)(2,1)S(1)} %copy-done.1), kind=kOutput, calls=%fused_computation.6 | convolution fusion | flops 2150628352 | bytes 8396800 | tf_op jit(solution)/shard_map/dot_general | solution.py:12
  47.2 13.2 %pmax.7 = f32[1024]{0:T(1024)S(1)} all-reduce(f32[1024]{0:T(1024)S(1)} %get-tuple-element.6), channel_id=1, replica_groups=mesh['grp'=4,'inner'=8] {'inner'}, use_global_device_ids=true, to_apply=%region_2.0 | all-reduce | flops 1024 | bytes 8192 | tf_op jit(solution)/shard_map/pmax | solution.py:53
  60.4 3.1 %fusion.1 = f32[1024]{0:T(1024)S(1)} fusion(f32[1024,1024]{0,1:T(8,128)} %get-tuple-element.7, f32[1024]{0:T(1024)S(1)} %pmax.7, f32[1024]{0:T(1024)S(1)} %broadcast_multiply_fusion), kind=kLoop, calls=%fused_computation.7 | loop fusion | flops 4193280 | bytes 4206592 | tf_op jit(solution)/shard_map/reduce_sum | solution.py:54
  63.5 15.4 %psum.35 = f32[1024]{0:T(1024)S(1)} all-reduce(f32[1024]{0:T(1024)S(1)} %fusion.1), channel_id=1, replica_groups=mesh['grp'=4,'inner'=8] {'inner'}, use_global_device_ids=true, to_apply=%region_4.0 | all-reduce | flops 1024 | bytes 8192 | tf_op jit(solution)/shard_map/psum | solution.py:54
  78.9 3.6 %convert_reduce_fusion = (f32[1024]{0:T(1024)S(1)}, bf16[1024,1024]{0,1:T(8,128)(2,1)S(1)}) fusion(f32[1024]{0:T(1024)S(1)} %psum.35, f32[1024]{0:T(1024)S(1)} %pmax.7, f32[1024,1024]{0,1:T(8,128)} %get-tuple-element.7, f32[1024]{0:T(1024)S(1)} %broadcast_multiply_fusion), kind=kLoop, calls=%fused_computation | loop fusion | flops 7339008 | bytes 6307840 | tf_op jit(solution)/shard_map/reduce_sum | solution.py:56
  82.5 0.0 copy-done.2
  82.5 4.3 %fusion.18 = f32[1024,1024]{1,0:T(8,128)} fusion(bf16[1024,1024]{0,1:T(8,128)(2,1)S(1)} %get-tuple-element.5, bf16[1024,1024]{1,0:T(8,128)(2,1)S(1)} %copy-done.2), kind=kOutput, calls=%fused_computation.37 | convolution fusion | flops 2147483648 | bytes 8388608 | tf_op jit(solution)/shard_map/dot_general | solution.py:57
  86.9 0.0 all-reduce.3.cloned.1.call-update
  86.9 0.0 all-reduce.5.cloned.1.call-start
  87.0 1.1 copy-done
  88.1 0.3 fusion.2
  88.4 2.9 %fusion.5 = (f32[1024]{0:T(1024)S(1)}, f32[1024,512]{0,1:T(8,128)S(1)}) fusion(f32[512]{0:T(512)S(1)} %broadcast_multiply_fusion.1, bf16[1024,1024]{1,0:T(8,128)(2,1)} %param.4, bf16[512,1024]{1,0:T(8,128)(2,1)S(1)} %copy-done), kind=kOutput, calls=%fused_computation.20 | convolution fusion | flops 1075313664 | bytes 5249024 | tf_op jit(solution)/shard_map/dot_general | solution.py:20
  91.3 0.5 fusion.7
  91.8 8.1 %psum.37 = f32[1024]{0:T(1024)S(1)} all-reduce(f32[1024]{0:T(1024)S(1)} %get-tuple-element.4), channel_id=1, replica_groups=mesh['grp'=4,'inner'=8] {'grp'}, use_global_device_ids=true, to_apply=%region_10.0 | all-reduce | flops 1024 | bytes 8192 | tf_op jit(solution)/shard_map/psum | solution.py:64
  99.9 89.3 %all-reduce.3.cloned.1.call-done = f32[1024,1024]{1,0:T(8,128)} async-done(((f32[1024,1024]{1,0:T(8,128)}), f32[1024,1024]{1,0:T(8,128)}) %all-reduce.3.cloned.1.call-update) | async-done | bytes 4194320 | tf_op jit(solution)/shard_map/psum | solution.py:64
  189.1 3.8 %add_divide_fusion = f32[1024,1024]{1,0:T(8,128)S(1)} fusion(f32[1024,1024]{1,0:T(8,128)} %all-reduce.3.cloned.1.call-done, bf16[512,1024]{1,0:T(8,128)(2,1)S(1)} %copy-done, f32[1024]{0:T(1024)S(1)} %broadcast_add_fusion, f32[1024,512]{0,1:T(8,128)S(1)} %get-tuple-element.9, f32[1024]{0:T(1024)S(1)} %fusion.7, f32[1024]{0:T(1024)S(1)} %get-tuple-element.8, ...), kind=kOutput, calls=%fused_computation.1 | convolution fusion | flops 1078460416 | bytes 11548672 | tf_op jit(solution)/shard_map/dot_general | solution.py:31
  192.9 0.0 copy-start.3
  192.9 1.3 fusion.6
  194.3 0.5 fusion.8
  194.8 0.8 convert_reduce_fusion.1
  195.6 2.6 fusion.9
  198.2 0.0 all-reduce.5.cloned.1.call-update
  198.2 13.8 %psum.39 = f32[512]{0:T(512)S(1)} all-reduce(f32[512]{0:T(512)S(1)} %get-tuple-element.2), channel_id=1, replica_groups=mesh['grp'=4,'inner'=8] {'inner'}, use_global_device_ids=true, to_apply=%region_15.0 | all-reduce | flops 512 | bytes 4096 | tf_op jit(solution)/shard_map/psum | solution.py:68
  212.1 49.9 %all-reduce.5.cloned.1.call-done = f32[512,1024]{1,0:T(8,128)} async-done(((f32[512,1024]{1,0:T(8,128)}), f32[512,1024]{1,0:T(8,128)}) %all-reduce.5.cloned.1.call-update) | async-done | bytes 2097168 | tf_op jit(solution)/shard_map/psum | solution.py:68
  261.9 3.4 %fusion.4 = f32[512,1024]{1,0:T(8,128)} fusion(f32[512,1024]{1,0:T(8,128)} %all-reduce.5.cloned.1.call-done, bf16[512,1024]{1,0:T(8,128)(2,1)S(1)} %copy-done, f32[512]{0:T(512)S(1)} %broadcast_add_fusion.1), kind=kLoop, calls=%fused_computation.12 | loop fusion | flops 2097152 | bytes 5244928 | tf_op jit(solution)/shard_map/div | solution.py:69
  (7 shorter events, 0.0 us)
Async XLA Ops:
  7.2 34.1 %copy-start.1 = (bf16[1024,1024]{1,0:T(8,128)(2,1)S(1)}, bf16[1024,1024]{1,0:T(8,128)(2,1)}, u32[]{:S(2)}) copy-start(bf16[1024,1024]{1,0:T(8,128)(2,1)} %param.4) | copy-start | bytes 6291460
  7.2 34.0 %all-gather.2.cloned.1.call-start = ((), (), s32[]{:S(2)}) async-start(), calls=%async_computation | async-start | bytes 2359296 | tf_op jit(solution)/shard_map/all_gather | solution.py:51
  7.9 181.2 %all-reduce.3.cloned.1.call-start = ((), (), s32[]{:S(2)}) async-start(), calls=%async_computation.1 | async-start | bytes 8388608 | tf_op jit(solution)/shard_map/psum | solution.py:64
  78.9 3.6 %copy-start.2 = (bf16[1024,1024]{1,0:T(8,128)(2,1)S(1)}, bf16[1024,1024]{1,0:T(8,128)(2,1)}, u32[]{:S(2)}) copy-start(bf16[1024,1024]{1,0:T(8,128)(2,1)} %all-gather.2.cloned.1.call-done) | copy-start | bytes 6291460
  86.9 1.2 copy-start
  86.9 175.0 %all-reduce.5.cloned.1.call-start = ((), (), s32[]{:S(2)}) async-start(), calls=%async_computation.2 | async-start | bytes 4194304 | tf_op jit(solution)/shard_map/psum | solution.py:68
  192.9 2.6 copy-start.3
Sparse Core Ops, SparseCore 0:
  9.6 31.5 all-gather.1
  87.0 102.0 all-reduce.2
  198.3 63.5 all-reduce.4
where the time goes:
time: 274 us; the launch traced here: 272 us
  waiting for transfers between devices  171 us (62%)
  blocking collectives  50.5 us (18%)
  matrix products  20.9 us (8%)
  other arithmetic  14.2 us (5%)
  between operations  13.8 us (5%)
    psum x1, waiting for transfers between devices, on_device(): moment, mass_sum = lax.psum((moment_local, mass_local), 'grp')  89.3 us
    psum x1, waiting for transfers between devices, on_device(): numerator, denominator = lax.psum((numerator, denominator), 'inner')  49.9 us
    all_gather x1, waiting for transfers between devices, on_device(): lax.all_gather(embeds, 'inner', axis=0, tiled=True)  31.2 us
    psum x1, blocking collectives, on_device(): lax.psum(jnp.sum(jnp.exp(scores - row_peaks[:, None]), axis=1), 'inner')  15.4 us
    psum x1, blocking collectives, on_device(): numerator, denominator = lax.psum((numerator, denominator), 'inner')  13.8 us
    pmax x1, blocking collectives, on_device(): row_peaks = lax.pmax(jnp.max(scores, axis=1), 'inner')  13.2 us
    psum x1, blocking collectives, on_device(): moment, mass_sum = lax.psum((moment_local, mass_local), 'grp')  8.08 us
    dot_general x1, matrix products, row_scores(): lax.dot_general(row_block, fine_cent, (((1,), (1,)), ((), ())), preferred...  5.98 us
  transfers between devices with their start and end apart: 3, of which 3 were waited for; matrix products, arithmetic and copies ran while one was open for 2% of the time, Pallas kernels for 0%

commit v1 on v0

v1 whole, which is shorter than its diff:
```python
import functools

import jax
import jax.numpy as jnp
from jax import lax
from jax.experimental import pallas as pl
from jax.experimental.pallas import tpu as pltpu
from jax.sharding import PartitionSpec as P

temper = 0.02
shrink = 1.0
anchor = 8.0
MESH = pl.DeviceIdType.MESH
F32 = jnp.float32
BF16 = jnp.bfloat16
NT = (((1,), (1,)), ((), ()))
TN = (((0,), (0,)), ((), ()))


def tile_of(n, most=256):
    return most if n % most == 0 else n


def ring_place(g, groups):
    half = groups // 2
    return jnp.where(g < half, g, 3 * half - 1 - g)


def gather_kernel(
    groups, inner, with_prior,
    e_ref, fine_ref, coarse_ref,
    moment_ref, mass_ref,
    rows, prob, sbuf, half_sq, mass, peak, stat,
    up_send, down_send, z_recv, ring_send, ring_recv, sib_send, sib_recv, stat_send, stat_recv,
):
    layers = inner // 2
    reach = groups // 2
    count = e_ref.shape[0]
    both = 2 * count
    part = count // 2
    width = e_ref.shape[1]
    kl = fine_ref.shape[0]
    kt = tile_of(kl)
    g = lax.axis_index("grp")
    i = lax.axis_index("inner")
    z = i // 2
    core = i % 2
    place = ring_place(g, groups)
    ahead = ring_place((place + 1) % groups, groups)
    behind = ring_place((place + groups - 1) % groups, groups)
    sibling = (g, 2 * z + 1 - core)

    barrier = pltpu.get_barrier_semaphore()
    for off in range(1, inner):
        pl.semaphore_signal(barrier, inc=1, device_id=(g, (i + off) % inner), device_id_type=MESH)
    for other in (ahead, behind):
        pl.semaphore_signal(barrier, inc=1, device_id=(other, i), device_id_type=MESH)
    pl.semaphore_wait(barrier, inner + 1)

    low = jnp.minimum(z, layers - 1 - z)
    side = jnp.where(2 * z < layers - 1, 1, -1)

    def layer_at(q):
        near = z + ((q + 1) // 2) * (1 - 2 * (q % 2))
        return jnp.where(q <= 2 * low, near, z + side * (q - low))

    def slots_of(h):
        if h == 0:
            return (0,)
        if h == reach:
            return (groups - 1,)
        return (2 * h - 1, 2 * h)

    def up_copy(zz):
        block = rows.at[zz, 0, core]
        return pltpu.make_async_remote_copy(
            block, block, up_send.at[zz], z_recv.at[zz], (g, i + 2), device_id_type=MESH)

    def down_copy(zz):
        block = rows.at[zz, 0, core]
        return pltpu.make_async_remote_copy(
            block, block, down_send.at[zz], z_recv.at[zz], (g, i - 2), device_id_type=MESH)

    def ring_copy(zz, hop, way):
        source = 0 if hop == 1 else 2 * (hop - 1) - 1 + way
        if hop < reach:
            src, dst = rows.at[zz, source, core], rows.at[zz, 2 * hop - 1 + way, core]
        else:
            piece = pl.ds(way * part, part)
            src, dst = rows.at[zz, source, core, piece], rows.at[zz, groups - 1, core, piece]
        return pltpu.make_async_remote_copy(
            src, dst, ring_send.at[way, zz, hop - 1], ring_recv.at[way, zz, hop - 1],
            (ahead if way == 0 else behind, i), device_id_type=MESH)

    def sib_copy(zz, slot):
        block = rows.at[zz, slot, core]
        return pltpu.make_async_remote_copy(
            block, block, sib_send.at[zz, slot], sib_recv.at[zz, slot], sibling, device_id_type=MESH)

    def sib_arrival(zz, slot):
        block = rows.at[zz, slot, 1 - core]
        return pltpu.make_async_remote_copy(
            block, block, sib_send.at[zz, slot], sib_recv.at[zz, slot], sibling, device_id_type=MESH)

    def goes_up(zz):
        return jnp.logical_and(zz <= z, z < layers - 1)

    def goes_down(zz):
        return jnp.logical_and(zz >= z, z > 0)

    def forward(h, q):
        zz = layer_at(q)
        if h == 0:
            @pl.when(q > 0)
            def _():
                up_copy(zz).wait_recv()

            @pl.when(goes_up(zz))
            def _():
                up_copy(zz).start()

            @pl.when(goes_down(zz))
            def _():
                down_copy(zz).start()
        else:
            for way in (0, 1):
                ring_copy(zz, h, way).wait_recv()
        if h < reach:
            for way in (0, 1):
                ring_copy(zz, h + 1, way).start()
        for slot in slots_of(h):
            sib_copy(zz, slot).start()

    def stat_copy(zz, h, peer):
        slots = slots_of(h)
        piece = stat.at[zz, i, pl.ds(slots[0], len(slots))]
        return pltpu.make_async_remote_copy(
            piece, piece, stat_send.at[zz, h], stat_recv.at[zz, h], (g, peer), device_id_type=MESH)

    def stat_all(zz, h):
        slots = slots_of(h)
        piece = stat.at[zz, pl.ds(0, inner - 1), pl.ds(slots[0], len(slots))]
        return pltpu.make_async_remote_copy(
            piece, piece, stat_send.at[zz, h], stat_recv.at[zz, h], (g, (i + 1) % inner), device_id_type=MESH)

    def score(h, q):
        zz = layer_at(q)
        for slot in slots_of(h):
            sib_arrival(zz, slot).wait_recv()
            block = rows[zz, slot].reshape(both, width)

            def first(t, top):
                ks = pl.ds(pl.multiple_of(t * kt, kt), kt)
                s = lax.dot_general(fine_ref[ks, :], block, NT, preferred_element_type=F32)
                s = s * (1.0 / temper) - half_sq[ks, :]
                sbuf[ks, :] = s
                return jnp.maximum(top, jnp.max(s, axis=0, keepdims=True))

            top = lax.fori_loop(0, kl // kt, first, jnp.full((1, both), -jnp.inf, F32))

            def second(t, total):
                ks = pl.ds(pl.multiple_of(t * kt, kt), kt)
                e = jnp.exp(sbuf[ks, :] - top)
                prob[zz, slot, ks, :] = e.astype(BF16)
                return total + jnp.sum(e, axis=0, keepdims=True)

            total = lax.fori_loop(0, kl // kt, second, jnp.zeros((1, both), F32))
            peak[zz, slot] = top
            stat[zz, i, slot] = top + jnp.log(total)
        for off in range(1, inner):
            stat_copy(zz, h, (i + off) % inner).start()

    def moments(h, u):
        items = []
        for zz in (layers // 2 - 1 - u, layers // 2 + u):
            stat_all(zz, h).wait_recv()
            for slot in slots_of(h):
                lse = stat[zz, :, slot]
                most = jnp.max(lse, axis=0)
                lse = most + jnp.log(jnp.sum(jnp.exp(lse - most[None]), axis=0))
                items.append((zz, slot, jnp.exp(peak[zz, slot] - lse)))

        def step(t, carry):
            ks = pl.ds(pl.multiple_of(t * kt, kt), kt)
            acc = moment_ref[ks, :]
            seen = mass[ks, :]
            for zz, slot, scale in items:
                resp = prob[zz, slot, ks, :].astype(F32) * scale
                seen = seen + resp
                acc = acc + jnp.dot(
                    resp.astype(BF16), rows[zz, slot].reshape(both, width), preferred_element_type=F32)
            moment_ref[ks, :] = acc
            mass[ks, :] = seen
            return carry

        lax.fori_loop(0, kl // kt, step, 0)

    rows[z, 0, core] = e_ref[...]
    forward(0, 0)

    def squares(t, carry):
        ks = pl.ds(pl.multiple_of(t * kt, kt), kt)
        f = fine_ref[ks, :].astype(F32)
        half_sq[ks, :] = jnp.broadcast_to(
            (0.5 / temper) * jnp.sum(f * f, axis=1, keepdims=True), (kt, both))
        mass[ks, :] = jnp.zeros((kt, both), F32)
        if not with_prior:
            moment_ref[ks, :] = jnp.zeros((kt, width), F32)
        return carry

    lax.fori_loop(0, kl // kt, squares, 0)
    if with_prior:
        c = coarse_ref[...].astype(F32)
        c_sq = jnp.broadcast_to(jnp.sum(c * c, axis=1, keepdims=True), (c.shape[0], 128))
        c_half = (0.5 / temper) * jnp.transpose(c_sq)[0:1, :]

        def prior(t, carry):
            ks = pl.ds(pl.multiple_of(t * kt, kt), kt)
            logits = lax.dot_general(fine_ref[ks, :], coarse_ref[...], NT, preferred_element_type=F32)
            logits = logits * (1.0 / temper) - c_half
            e = jnp.exp(logits - jnp.max(logits, axis=1, keepdims=True))
            parent = (e / jnp.sum(e, axis=1, keepdims=True)).astype(BF16)
            moment_ref[ks, :] = shrink * jnp.dot(parent, coarse_ref[...], preferred_element_type=F32)
            return carry

        lax.fori_loop(0, kl // kt, prior, 0)

    def turn(t, carry):
        for h in range(reach + 1):
            q = t - h

            @pl.when(jnp.logical_and(jnp.logical_and(q >= 0, q < layers), t > 0))
            def _():
                forward(h, q)

        for h in range(reach + 1):
            q = t - h

            @pl.when(jnp.logical_and(q >= 0, q < layers))
            def _():
                score(h, q)

        for h in range(reach + 1):
            u = t - h - 1 - layers // 2

            @pl.when(jnp.logical_and(u >= 0, u < layers // 2))
            def _():
                moments(h, u)

        return carry

    lax.fori_loop(0, layers + reach + 1, turn, 0)

    mass_ref[...] = jnp.broadcast_to(jnp.sum(mass[...], axis=1, keepdims=True), mass_ref.shape)

    def drain(zz, carry):
        @pl.when(goes_up(zz))
        def _():
            up_copy(zz).wait_send()

        @pl.when(goes_down(zz))
        def _():
            down_copy(zz).wait_send()

        for h in range(reach + 1):
            if h < reach:
                for way in (0, 1):
                    ring_copy(zz, h + 1, way).wait_send()
            for slot in slots_of(h):
                sib_copy(zz, slot).wait_send()
            stat_all(zz, h).wait_send()
        return carry

    lax.fori_loop(0, layers, drain, 0)


def gathered_moments(groups, inner, number, embeds, fine, coarse):
    layers, reach = inner // 2, groups // 2
    count, width = embeds.shape
    kl = fine.shape[0]
    both = 2 * count
    dma = pltpu.SemaphoreType.DMA
    vm = pl.BlockSpec(memory_space=pltpu.VMEM)
    total = groups * inner * count
    return pl.pallas_call(
        functools.partial(gather_kernel, groups, inner, number == 0),
        out_shape=(
            jax.ShapeDtypeStruct((kl, width), F32),
            jax.ShapeDtypeStruct((kl, 128), F32),
        ),
        in_specs=[vm] * 3,
        out_specs=(vm, vm),
        scratch_shapes=[
            pltpu.VMEM((layers, groups, 2, count, width), BF16),
            pltpu.VMEM((layers, groups, kl, both), BF16),
            pltpu.VMEM((kl, both), F32),
            pltpu.VMEM((kl, both), F32),
            pltpu.VMEM((kl, both), F32),
            pltpu.VMEM((layers, groups, 1, both), F32),
            pltpu.VMEM((layers, inner, groups, 1, both), F32),
            dma((layers,)), dma((layers,)), dma((layers,)),
            dma((2, layers, reach)), dma((2, layers, reach)),
            dma((layers, groups)), dma((layers, groups)),
            dma((layers, reach + 1)), dma((layers, reach + 1)),
        ],
        compiler_params=pltpu.CompilerParams(
            collective_id=number, has_side_effects=True, vmem_limit_bytes=56 * 1024 * 1024),
        cost_estimate=pl.CostEstimate(
            flops=4 * total * kl * width, bytes_accessed=8 * kl * width, transcendentals=total * kl),
    )(embeds, fine, coarse)


def coarse_softmax(fine_low, coarse_cent, coarse_sq):
    logits = (lax.dot_general(fine_low, coarse_cent, NT, preferred_element_type=F32) - 0.5 * coarse_sq) / temper
    shifted = jnp.exp(logits - jnp.max(logits, axis=1, keepdims=True))
    return shifted / jnp.sum(shifted, axis=1, keepdims=True)


def on_device(groups, inner, embeds, fine_centroids, coarse_centroids):
    count, width = embeds.shape
    kl = fine_centroids.shape[0]
    rounds = 1
    while groups * inner * (count // rounds) * (width + kl) * 2 > 34 * 1024 * 1024:
        rounds *= 2
    step = count // rounds
    moment, mass = None, None
    for r in range(rounds):
        m, s = gathered_moments(
            groups, inner, r, embeds[r * step:(r + 1) * step], fine_centroids, coarse_centroids)
        moment = m if moment is None else moment + m
        mass = s if mass is None else mass + s
    weight = mass[:, :1] + shrink
    fine_update = moment / weight
    fine_low = fine_update.astype(BF16)
    coarse_sq = jnp.sum(jnp.square(coarse_centroids.astype(F32)), axis=1)
    share = (coarse_softmax(fine_low, coarse_centroids, coarse_sq) * weight).astype(BF16)
    numerator = lax.dot_general(share, fine_low, TN, preferred_element_type=F32)
    denominator = jnp.sum(share, axis=0, dtype=F32)
    numerator, denominator = lax.psum((numerator, denominator), "inner")
    coarse_update = (numerator + anchor * coarse_centroids.astype(F32)) / (denominator[:, None] + anchor)
    return (fine_update, coarse_update)


def solution(mesh):
    return jax.shard_map(
        functools.partial(on_device, mesh.shape["grp"], mesh.shape["inner"]),
        mesh=mesh,
        in_specs=(P(("grp", "inner"), None), P("inner", None), P()),
        out_specs=(P("inner", None), P()),
        check_vma=False,
    )
```

time: 274 us -> 165 us (0.60)
  waiting for transfers between devices: 171 us -> 47.7 us
  Pallas kernels: 0 us -> 72.9 us
  blocking collectives: 50.5 us -> 13.7 us
  matrix products: 20.9 us -> 3.89 us
  other arithmetic: 14.2 us -> 10.1 us
    psum x1 -> x0, waiting for transfers between devices: 89.3 us -> none  [on_device(): moment, mass_sum = lax.psum((moment_local, mass_local), 'grp')]
    pallas_call x0 -> x1, Pallas kernels: none -> 72.9 us  [gathered_moments(): pl.pallas_call(functools.partial(gather_kernel, groups, inner, number ==...]
    all_gather x1 -> x0, waiting for transfers between devices: 31.2 us -> none  [on_device(): lax.all_gather(embeds, 'inner', axis=0, tiled=True)]
    psum x2 -> x0, blocking collectives: 23.5 us -> none  [the longest x1 15.4 us: on_device(): lax.psum(jnp.sum(jnp.exp(scores - row_peaks[:, None]), axis=1), 'inner')]
    dot_general x6 -> x2, matrix products: 20.9 us -> 3.89 us  [the longest x1 2.59 us: on_device(): numerator = lax.dot_general(share, fine_low, TN, preferred_element_type=F32)]
    pmax x1 -> x0, blocking collectives: 13.2 us -> none  [on_device(): row_peaks = lax.pmax(jnp.max(scores, axis=1), 'inner')]
    reduce_sum x5 -> x2, other arithmetic: 9.85 us -> 2.3 us  [the longest x1 1.5 us: on_device(): coarse_sq = jnp.sum(jnp.square(coarse_centroids.astype(F32)), axis=1)]
    div x1 -> x2, other arithmetic: 3.36 us -> 6.07 us  [the longest x1 3.36 us: on_device(): (numerator + anchor * coarse_centroids.astype(F32)) / (denominator[:, Non...]
  transfers between devices with their start and end apart: 3 -> 1, of which waited for: 3 -> 1; matrix products, arithmetic and copies ran while one was open for 2% -> 0% of each run, Pallas kernels for 0% -> 0%
where the time goes in v1:
time: 165 us; the launch traced here: 162 us
  Pallas kernels  72.9 us (44%)
  waiting for transfers between devices  47.7 us (29%)
  between operations  14.1 us (9%)
  blocking collectives  13.7 us (8%)
  other arithmetic  10.1 us (6%)
  matrix products  3.89 us (2%)
    pallas_call x1, Pallas kernels, gathered_moments(): pl.pallas_call(functools.partial(gather_kernel, groups, inner, number ==...  72.9 us
    psum x1, waiting for transfers between devices, on_device(): numerator, denominator = lax.psum((numerator, denominator), 'inner')  47.7 us
    psum x1, blocking collectives, on_device(): numerator, denominator = lax.psum((numerator, denominator), 'inner')  13.7 us
    div x1, other arithmetic, on_device(): (numerator + anchor * coarse_centroids.astype(F32)) / (denominator[:, Non...  3.36 us
  transfers between devices with their start and end apart: 1, of which 1 were waited for; matrix products, arithmetic and copies ran while one was open for 0% of the time, Pallas kernels for 0%

profile of v1, /device:TPU:1, one launch (start us, length us, event | category | flops | bytes accessed | tf_op | source)
XLA Modules:
  0.0 162.4 jit_solution(4861340983368325404)
XLA Ops:
  7.2 0.0 all-reduce.2.cloned.1.call-start
  7.2 1.5 fusion
  8.7 72.9 %shard_map.50 = (f32[1024,1024]{1,0:T(8,128)}, f32[1024,128]{1,0:T(8,128)}) custom-call(bf16[128,1024]{1,0:T(8,128)(2,1)} %e_ref.1, bf16[1024,1024]{1,0:T(8,128)(2,1)} %fine_ref.1, bf16[512,1024]{1,0:T(8,128)(2,1)} %coarse_ref.1), custom_call_target="tpu_custom_call" | custom-call | flops 17179869184 | bytes 8388608 | tf_op jit(solution)/shard_map/pallas_call | solution.py:285
  81.6 1.2 add_reduce_fusion
  82.9 0.0 copy-start
  82.9 2.7 %broadcast_divide_fusion = f32[1024,1024]{1,0:T(8,128)S(1)} fusion(f32[1024,1024]{1,0:T(8,128)} %get-tuple-element.4, f32[1024]{0:T(1024)S(1)} %add_reduce_fusion), kind=kLoop, calls=%fused_computation.9 | loop fusion | flops 1048576 | bytes 8392704 | tf_op jit(solution)/shard_map/div | solution.py:333
  85.6 0.0 copy-done
  85.6 0.0 copy-start.1
  85.6 1.3 fusion.3
  86.9 0.5 fusion.4
  87.4 0.8 convert_reduce_fusion
  88.2 0.0 copy-done.1
  88.2 2.6 %fusion.5 = f32[512,1024]{1,0:T(8,128)} fusion(bf16[1024,512]{0,1:T(8,128)(2,1)S(1)} %get-tuple-element.7, f32[1024,1024]{1,0:T(8,128)S(1)} %broadcast_divide_fusion), kind=kOutput, calls=%fused_computation.12 | convolution fusion | flops 1074790400 | bytes 7340032 | tf_op jit(solution)/shard_map/dot_general | solution.py:337
  90.8 0.0 all-reduce.2.cloned.1.call-update
  90.8 13.7 %psum.15 = f32[512]{0:T(512)S(1)} all-reduce(f32[512]{0:T(512)S(1)} %get-tuple-element.6), channel_id=1, replica_groups=mesh['grp'=4,'inner'=8] {'inner'}, use_global_device_ids=true, to_apply=%region_5.0 | all-reduce | flops 512 | bytes 4096 | tf_op jit(solution)/shard_map/psum | solution.py:339
  104.5 47.7 %all-reduce.2.cloned.1.call-done = f32[512,1024]{1,0:T(8,128)} async-done(((f32[512,1024]{1,0:T(8,128)}), f32[512,1024]{1,0:T(8,128)}) %all-reduce.2.cloned.1.call-update) | async-done | bytes 2097168 | tf_op jit(solution)/shard_map/psum | solution.py:339
  152.2 3.4 %fusion.2 = f32[512,1024]{1,0:T(8,128)} fusion(f32[512,1024]{1,0:T(8,128)} %all-reduce.2.cloned.1.call-done, bf16[512,1024]{1,0:T(8,128)(2,1)S(1)} %copy-done, f32[512]{0:T(512)S(1)} %broadcast_add_fusion), kind=kLoop, calls=%fused_computation.4 | loop fusion | flops 2097152 | bytes 5244928 | tf_op jit(solution)/shard_map/div | solution.py:340
  (2 shorter events, 0.0 us)
Async XLA Ops:
  7.2 145.1 %all-reduce.2.cloned.1.call-start = ((), (), s32[]{:S(2)}) async-start(), calls=%async_computation | async-start | bytes 4194304 | tf_op jit(solution)/shard_map/psum | solution.py:339
  82.9 2.7 %copy-start = (bf16[512,1024]{1,0:T(8,128)(2,1)S(1)}, bf16[512,1024]{1,0:T(8,128)(2,1)}, u32[]{:S(2)}) copy-start(bf16[512,1024]{1,0:T(8,128)(2,1)} %coarse_ref.1) | copy-start | bytes 3145732
  85.6 2.6 %copy-start.1 = (f32[1024,1024]{1,0:T(8,128)}, f32[1024,1024]{1,0:T(8,128)S(1)}, u32[]{:S(2)}) copy-start(f32[1024,1024]{1,0:T(8,128)S(1)} %broadcast_divide_fusion) | copy-start | bytes 12582916
Sparse Core Ops, SparseCore 0:
  90.9 61.2 all-reduce.1

commit v2 on v1

--- a/solution.py
+++ b/solution.py
@@ -14,7 +14,6 @@
 F32 = jnp.float32
 BF16 = jnp.bfloat16
 NT = (((1,), (1,)), ((), ()))
-TN = (((0,), (0,)), ((), ()))
 
 
 def tile_of(n, most=256):
@@ -27,12 +26,20 @@
 
 
 def gather_kernel(
-    groups, inner, with_prior,
-    e_ref, fine_ref, coarse_ref,
-    moment_ref, mass_ref,
-    rows, prob, sbuf, half_sq, mass, peak, stat,
-    up_send, down_send, z_recv, ring_send, ring_recv, sib_send, sib_recv, stat_send, stat_recv,
+    groups, inner, first_round, last_round, *refs,
 ):
+    refs = list(refs)
+    e_ref, fine_ref, coarse_ref = refs[:3]
+    del refs[:3]
+    if not first_round:
+        moment_in, mass_in = refs[:2]
+        del refs[:2]
+    moment_ref, mass_ref = refs[:2]
+    del refs[:2]
+    if last_round:
+        coarse_out = refs.pop(0)
+    (rows, prob, half_sq, mass, peak, stat,
+     up_send, down_send, z_recv, ring_send, ring_recv, sib_send, sib_recv, stat_send, stat_recv) = refs[:15]
     layers = inner // 2
     reach = groups // 2
     count = e_ref.shape[0]
@@ -41,6 +48,7 @@
     width = e_ref.shape[1]
     kl = fine_ref.shape[0]
     kt = tile_of(kl)
+    nt = tile_of(width)
     g = lax.axis_index("grp")
     i = lax.axis_index("inner")
     z = i // 2
@@ -53,9 +61,9 @@
     barrier = pltpu.get_barrier_semaphore()
     for off in range(1, inner):
         pl.semaphore_signal(barrier, inc=1, device_id=(g, (i + off) % inner), device_id_type=MESH)
-    for other in (ahead, behind):
-        pl.semaphore_signal(barrier, inc=1, device_id=(other, i), device_id_type=MESH)
-    pl.semaphore_wait(barrier, inner + 1)
+    for off in range(1, groups):
+        pl.semaphore_signal(barrier, inc=1, device_id=((g + off) % groups, i), device_id_type=MESH)
+    pl.semaphore_wait(barrier, inner + groups - 2)
 
     low = jnp.minimum(z, layers - 1 - z)
     side = jnp.where(2 * z < layers - 1, 1, -1)
@@ -149,22 +157,12 @@
             sib_arrival(zz, slot).wait_recv()
             block = rows[zz, slot].reshape(both, width)
 
-            def first(t, top):
-                ks = pl.ds(pl.multiple_of(t * kt, kt), kt)
-                s = lax.dot_general(fine_ref[ks, :], block, NT, preferred_element_type=F32)
-                s = s * (1.0 / temper) - half_sq[ks, :]
-                sbuf[ks, :] = s
-                return jnp.maximum(top, jnp.max(s, axis=0, keepdims=True))
-
-            top = lax.fori_loop(0, kl // kt, first, jnp.full((1, both), -jnp.inf, F32))
-
-            def second(t, total):
-                ks = pl.ds(pl.multiple_of(t * kt, kt), kt)
-                e = jnp.exp(sbuf[ks, :] - top)
-                prob[zz, slot, ks, :] = e.astype(BF16)
-                return total + jnp.sum(e, axis=0, keepdims=True)
-
-            total = lax.fori_loop(0, kl // kt, second, jnp.zeros((1, both), F32))
+            s = lax.dot_general(fine_ref[...], block, NT, preferred_element_type=F32)
+            s = s * (1.0 / temper) - half_sq[...]
+            top = jnp.max(s, axis=0, keepdims=True)
+            e = jnp.exp(s - top)
+            prob[zz, slot] = e.astype(BF16)
+            total = jnp.sum(e, axis=0, keepdims=True)
             peak[zz, slot] = top
             stat[zz, i, slot] = top + jnp.log(total)
         for off in range(1, inner):
@@ -180,20 +178,28 @@
                 lse = most + jnp.log(jnp.sum(jnp.exp(lse - most[None]), axis=0))
                 items.append((zz, slot, jnp.exp(peak[zz, slot] - lse)))
 
-        def step(t, carry):
+        def scaled(t, carry):
             ks = pl.ds(pl.multiple_of(t * kt, kt), kt)
-            acc = moment_ref[ks, :]
             seen = mass[ks, :]
             for zz, slot, scale in items:
                 resp = prob[zz, slot, ks, :].astype(F32) * scale
                 seen = seen + resp
-                acc = acc + jnp.dot(
-                    resp.astype(BF16), rows[zz, slot].reshape(both, width), preferred_element_type=F32)
-            moment_ref[ks, :] = acc
+                prob[zz, slot, ks, :] = resp.astype(BF16)
             mass[ks, :] = seen
             return carry
 
-        lax.fori_loop(0, kl // kt, step, 0)
+        lax.fori_loop(0, kl // kt, scaled, 0)
+
+        def step(t, carry):
+            ds = pl.ds(pl.multiple_of(t * nt, nt), nt)
+            acc = moment_ref[:, ds]
+            for zz, slot, scale in items:
+                acc = acc + jnp.dot(
+                    prob[zz, slot], rows[zz, slot, :, :, ds].reshape(both, nt), preferred_element_type=F32)
+            moment_ref[:, ds] = acc
+            return carry
+
+        lax.fori_loop(0, width // nt, step, 0)
 
     rows[z, 0, core] = e_ref[...]
     forward(0, 0)
@@ -204,12 +210,12 @@
         half_sq[ks, :] = jnp.broadcast_to(
             (0.5 / temper) * jnp.sum(f * f, axis=1, keepdims=True), (kt, both))
         mass[ks, :] = jnp.zeros((kt, both), F32)
-        if not with_prior:
-            moment_ref[ks, :] = jnp.zeros((kt, width), F32)
+        if not first_round:
+            moment_ref[ks, :] = moment_in[ks, :]
         return carry
 
     lax.fori_loop(0, kl // kt, squares, 0)
-    if with_prior:
+    if first_round:
         c = coarse_ref[...].astype(F32)
         c_sq = jnp.broadcast_to(jnp.sum(c * c, axis=1, keepdims=True), (c.shape[0], 128))
         c_half = (0.5 / temper) * jnp.transpose(c_sq)[0:1, :]
@@ -226,20 +232,22 @@
         lax.fori_loop(0, kl // kt, prior, 0)
 
     def turn(t, carry):
-        for h in range(reach + 1):
+        def gated(h, work):
             q = t - h
 
-            @pl.when(jnp.logical_and(jnp.logical_and(q >= 0, q < layers), t > 0))
+            @pl.when(jnp.logical_and(q >= 0, q < layers))
+            def _():
+                work(h, q)
+
+        def forward_later(h, q):
+            @pl.when(t > 0)
             def _():
                 forward(h, q)
 
-        for h in range(reach + 1):
-            q = t - h
-
-            @pl.when(jnp.logical_and(q >= 0, q < layers))
-            def _():
-                score(h, q)
-
+        for h in (0, 1):
+            gated(h, forward_later)
+        for h in (0, 1):
+            gated(h, score)
         for h in range(reach + 1):
             u = t - h - 1 - layers // 2
 
@@ -247,11 +255,19 @@
             def _():
                 moments(h, u)
 
+        for h in range(2, reach + 1):
+            gated(h, forward)
+            gated(h, score)
         return carry
 
     lax.fori_loop(0, layers + reach + 1, turn, 0)
 
-    mass_ref[...] = jnp.broadcast_to(jnp.sum(mass[...], axis=1, keepdims=True), mass_ref.shape)
+    heavy = jnp.broadcast_to(jnp.sum(mass[...], axis=1, keepdims=True), mass_ref.shape)
+    if not first_round:
+        heavy = heavy + mass_in[...]
+    mass_ref[...] = heavy
+    if last_round:
+        finish(groups, inner, coarse_ref, moment_ref, mass_ref, coarse_out, *refs[15:])
 
     def drain(zz, carry):
         @pl.when(goes_up(zz))
@@ -274,46 +290,211 @@
     lax.fori_loop(0, layers, drain, 0)
 
 
-def gathered_moments(groups, inner, number, embeds, fine, coarse):
+def shares_of(groups, inner, coarse_rows):
+    piece = 16
+    owners = min(inner // 2, coarse_rows // (groups * 2 * piece))
+    return piece, owners
+
+
+def finish(
+    groups, inner, coarse_ref, moment_ref, mass_ref, coarse_out,
+    fine_low, share, out1, in1, out2, in2, res,
+    sem1, send2, recv2, send3, recv3, send4, recv4, send5, recv5,
+):
+    layers = inner // 2
+    kl, width = moment_ref.shape
+    coarse_rows = coarse_ref.shape[0]
+    piece, owners = shares_of(groups, inner, coarse_rows)
+    own_rows = 2 * owners * piece
+    kt = tile_of(kl)
+    g = lax.axis_index("grp")
+    i = lax.axis_index("inner")
+    z = i // 2
+    core = i % 2
+    sibling = (g, 2 * z + 1 - core)
+
+    c = coarse_ref[...].astype(F32)
+    c_half = (0.5 / temper) * jnp.sum(c * c, axis=1, keepdims=True)
+
+    def child(t, carry):
+        ks = pl.ds(pl.multiple_of(t * kt, kt), kt)
+        weight = mass_ref[ks, :] + shrink
+        new = moment_ref[ks, :] / weight[:, 0:1]
+        moment_ref[ks, :] = new
+        low = new.astype(BF16)
+        fine_low[ks, :] = low
+        logits = lax.dot_general(coarse_ref[...], low, NT, preferred_element_type=F32)
+        logits = logits * (1.0 / temper) - c_half
+        e = jnp.exp(logits - jnp.max(logits, axis=0, keepdims=True))
+        scale = jnp.transpose(weight)[0:1, :] / jnp.sum(e, axis=0, keepdims=True)
+        share[:, ks] = (e * scale).astype(BF16)
+        return carry
+
+    lax.fori_loop(0, kl // kt, child, 0)
+
+    mine = share[pl.ds(pl.multiple_of(g * own_rows, own_rows), own_rows), :]
+    numerator = jnp.dot(mine, fine_low[...], preferred_element_type=F32)
+    den = jnp.broadcast_to(jnp.sum(mine.astype(F32), axis=1, keepdims=True), (own_rows, 128))
+
+    def packed(total):
+        high = total.astype(BF16)
+        rest = (total - high.astype(F32)).astype(BF16)
+        lane = lax.broadcasted_iota(jnp.int32, total.shape, total.ndim - 1)
+        return jnp.where(lane < 64, high.astype(F32), rest.astype(F32)).astype(BF16)
+
+    def unpacked(pair):
+        return pair[..., 0:1] + pair[..., 64:65]
+
+    shape = (2, owners, piece)
+    out1[:, :, :, :width] = numerator.astype(BF16).reshape(*shape, width)
+    out1[:, :, :, width:] = packed(den).reshape(*shape, 128)
+    swap = pltpu.make_async_remote_copy(
+        out1.at[1 - core], in1, sem1.at[0], sem1.at[1], sibling, device_id_type=MESH)
+    swap.start()
+    swap.wait_recv()
+    a, b = out1[core].astype(F32), in1[...].astype(F32)
+    out2[:, :, :width] = (a[..., :width] + b[..., :width]).astype(BF16)
+    both_den = jnp.broadcast_to(unpacked(a[..., width:]) + unpacked(b[..., width:]), (owners, piece, 128))
+    out2[:, :, width:] = packed(both_den)
+
+    def part_copy(zo):
+        return pltpu.make_async_remote_copy(
+            out2.at[zo], in2.at[z], send2.at[zo], recv2.at[z], (g, 2 * zo + core), device_id_type=MESH)
+
+    def part_arrival(zs):
+        return pltpu.make_async_remote_copy(
+            out2.at[0], in2.at[zs], send2.at[0], recv2.at[zs], (g, 2 * zs + core), device_id_type=MESH)
+
+    def done_copy(zt):
+        block = res.at[g, core, z]
+        return pltpu.make_async_remote_copy(
+            block, block, send3.at[zt], recv3.at[z], (g, 2 * zt + core), device_id_type=MESH)
+
+    def done_arrival(zs):
+        block = res.at[g, core, zs]
+        return pltpu.make_async_remote_copy(
+            block, block, send3.at[zs], recv3.at[zs], (g, 2 * zs + core), device_id_type=MESH)
+
+    def when_owner(zo, work):
+        if owners == layers:
+            work()
+        else:
+            pl.when(zo < owners)(work)
+
+    for off in range(1, layers):
+        zo = (z + off) % layers
+        when_owner(zo, lambda zo=zo: part_copy(zo).start())
+
+    def own():
+        for off in range(1, layers):
+            part_arrival((z + off) % layers).wait_recv()
+        in2[z] = out2[z]
+        got = in2[...].astype(F32)
+        num = jnp.sum(got[..., :width], axis=0)
+        total = jnp.sum(unpacked(got[..., width:]), axis=0)
+        at = pl.multiple_of(g * own_rows + (core * owners + z) * piece, piece)
+        old = coarse_ref[pl.ds(at, piece), :].astype(F32)
+        res[g, core, z] = ((num + anchor * old) / (total + anchor)).astype(BF16)
+        for off in range(1, layers):
+            done_copy((z + off) % layers).start()
+
+    when_owner(z, own)
+    for off in range(1, layers):
+        zo = (z + off) % layers
+        when_owner(zo, lambda zo=zo: done_arrival(zo).wait_recv())
+
+    def group_copy(gt):
+        block = res.at[g, core]
+        return pltpu.make_async_remote_copy(
+            block, block, send4.at[gt], recv4.at[g], (gt, i), device_id_type=MESH)
+
+    def group_arrival(gs):
+        block = res.at[gs, core]
+        return pltpu.make_async_remote_copy(
+            block, block, send4.at[gs], recv4.at[gs], (gs, i), device_id_type=MESH)
+
+    def over(gs):
+        block = res.at[gs, core]
+        return pltpu.make_async_remote_copy(
+            block, block, send5.at[gs], recv5.at[gs], sibling, device_id_type=MESH)
+
+    def over_arrival(gs):
+        block = res.at[gs, 1 - core]
+        return pltpu.make_async_remote_copy(
+            block, block, send5.at[gs], recv5.at[gs], sibling, device_id_type=MESH)
+
+    for off in range(1, groups):
+        group_copy((g + off) % groups).start()
+    over(g).start()
+    for off in range(1, groups):
+        gs = (g + off) % groups
+        group_arrival(gs).wait_recv()
+        over(gs).start()
+    for gs in range(groups):
+        over_arrival(gs).wait_recv()
+    coarse_out[...] = res[...].reshape(coarse_rows, width)
+
+    swap.wait_send()
+    for off in range(1, layers):
+        zo = (z + off) % layers
+        when_owner(zo, lambda zo=zo: part_copy(zo).wait_send())
+        when_owner(z, lambda zo=zo: done_copy(zo).wait_send())
+    for off in range(1, groups):
+        group_copy((g + off) % groups).wait_send()
+    for gs in range(groups):
+        over(gs).wait_send()
+
+
+def gathered_moments(groups, inner, number, rounds, embeds, fine, coarse, before):
     layers, reach = inner // 2, groups // 2
     count, width = embeds.shape
     kl = fine.shape[0]
+    coarse_rows = coarse.shape[0]
     both = 2 * count
     dma = pltpu.SemaphoreType.DMA
     vm = pl.BlockSpec(memory_space=pltpu.VMEM)
     total = groups * inner * count
+    last = number == rounds - 1
+    out_shape = [jax.ShapeDtypeStruct((kl, width), F32), jax.ShapeDtypeStruct((kl, 128), F32)]
+    scratch = [
+        pltpu.VMEM((layers, groups, 2, count, width), BF16),
+        pltpu.VMEM((layers, groups, kl, both), BF16),
+        pltpu.VMEM((kl, both), F32),
+        pltpu.VMEM((kl, both), F32),
+        pltpu.VMEM((layers, groups, 1, both), F32),
+        pltpu.VMEM((layers, inner, groups, 1, both), F32),
+        dma((layers,)), dma((layers,)), dma((layers,)),
+        dma((2, layers, reach)), dma((2, layers, reach)),
+        dma((layers, groups)), dma((layers, groups)),
+        dma((layers, reach + 1)), dma((layers, reach + 1)),
+    ]
+    if last:
+        piece, owners = shares_of(groups, inner, coarse_rows)
+        wide = width + 128
+        out_shape.append(jax.ShapeDtypeStruct((coarse_rows, width), BF16))
+        scratch += [
+            pltpu.VMEM((kl, width), BF16),
+            pltpu.VMEM((coarse_rows, kl), BF16),
+            pltpu.VMEM((2, owners, piece, wide), BF16),
+            pltpu.VMEM((owners, piece, wide), BF16),
+            pltpu.VMEM((owners, piece, wide), BF16),
+            pltpu.VMEM((layers, piece, wide), BF16),
+            pltpu.VMEM((groups, 2, owners, piece, width), BF16),
+            dma((2,)), dma((layers,)), dma((layers,)), dma((layers,)), dma((layers,)),
+            dma((groups,)), dma((groups,)), dma((groups,)), dma((groups,)),
+        ]
+    args = (embeds, fine, coarse, *before)
     return pl.pallas_call(
-        functools.partial(gather_kernel, groups, inner, number == 0),
-        out_shape=(
-            jax.ShapeDtypeStruct((kl, width), F32),
-            jax.ShapeDtypeStruct((kl, 128), F32),
-        ),
-        in_specs=[vm] * 3,
-        out_specs=(vm, vm),
-        scratch_shapes=[
-            pltpu.VMEM((layers, groups, 2, count, width), BF16),
-            pltpu.VMEM((layers, groups, kl, both), BF16),
-            pltpu.VMEM((kl, both), F32),
-            pltpu.VMEM((kl, both), F32),
-            pltpu.VMEM((kl, both), F32),
-            pltpu.VMEM((layers, groups, 1, both), F32),
-            pltpu.VMEM((layers, inner, groups, 1, both), F32),
-            dma((layers,)), dma((layers,)), dma((layers,)),
-            dma((2, layers, reach)), dma((2, layers, reach)),
-            dma((layers, groups)), dma((layers, groups)),
-            dma((layers, reach + 1)), dma((layers, reach + 1)),
-        ],
+        functools.partial(gather_kernel, groups, inner, number == 0, last),
+        out_shape=out_shape,
+        in_specs=[vm] * len(args),
+        out_specs=[vm] * len(out_shape),
+        scratch_shapes=scratch,
         compiler_params=pltpu.CompilerParams(
-            collective_id=number, has_side_effects=True, vmem_limit_bytes=56 * 1024 * 1024),
+            collective_id=number, has_side_effects=True, vmem_limit_bytes=60 * 1024 * 1024),
         cost_estimate=pl.CostEstimate(
             flops=4 * total * kl * width, bytes_accessed=8 * kl * width, transcendentals=total * kl),
-    )(embeds, fine, coarse)
-
-
-def coarse_softmax(fine_low, coarse_cent, coarse_sq):
-    logits = (lax.dot_general(fine_low, coarse_cent, NT, preferred_element_type=F32) - 0.5 * coarse_sq) / temper
-    shifted = jnp.exp(logits - jnp.max(logits, axis=1, keepdims=True))
-    return shifted / jnp.sum(shifted, axis=1, keepdims=True)
+    )(*args)
 
 
 def on_device(groups, inner, embeds, fine_centroids, coarse_centroids):
@@ -323,22 +504,12 @@
     while groups * inner * (count // rounds) * (width + kl) * 2 > 34 * 1024 * 1024:
         rounds *= 2
     step = count // rounds
-    moment, mass = None, None
+    found = ()
     for r in range(rounds):
-        m, s = gathered_moments(
-            groups, inner, r, embeds[r * step:(r + 1) * step], fine_centroids, coarse_centroids)
-        moment = m if moment is None else moment + m
-        mass = s if mass is None else mass + s
-    weight = mass[:, :1] + shrink
-    fine_update = moment / weight
-    fine_low = fine_update.astype(BF16)
-    coarse_sq = jnp.sum(jnp.square(coarse_centroids.astype(F32)), axis=1)
-    share = (coarse_softmax(fine_low, coarse_centroids, coarse_sq) * weight).astype(BF16)
-    numerator = lax.dot_general(share, fine_low, TN, preferred_element_type=F32)
-    denominator = jnp.sum(share, axis=0, dtype=F32)
-    numerator, denominator = lax.psum((numerator, denominator), "inner")
-    coarse_update = (numerator + anchor * coarse_centroids.astype(F32)) / (denominator[:, None] + anchor)
-    return (fine_update, coarse_update)
+        found = gathered_moments(
+            groups, inner, r, rounds, embeds[r * step:(r + 1) * step], fine_centroids, coarse_centroids, found[:2])
+    fine_update, _, coarse_update = found
+    return (fine_update, coarse_update.astype(F32))
 
 
 def solution(mesh):

time: 165 us -> 110 us (0.67); the launches traced: 162 us -> 109 us
  waiting for transfers between devices: 47.7 us -> 0 us
  Pallas kernels: 72.9 us -> 101 us
  blocking collectives: 13.7 us -> 0 us
  between operations: 14.1 us -> 0.64 us
  other arithmetic: 10.1 us -> 2.79 us
  local copies, waits for them, and re-layouts: 0.01 us -> 4.79 us
  matrix products: 3.89 us -> 0 us
    psum x1 -> x0, waiting for transfers between devices: 47.7 us -> none  [on_device(): numerator, denominator = lax.psum((numerator, denominator), 'inner')]
    pallas_call x1, Pallas kernels: 72.9 us -> 101 us  [gathered_moments(): pl.pallas_call(functools.partial(gather_kernel, groups, inner, number ==...]
    psum x1 -> x0, blocking collectives: 13.7 us -> none  [on_device(): numerator, denominator = lax.psum((numerator, denominator), 'inner')]
    div x2 -> x0, other arithmetic: 6.07 us -> none  [the longest x1 3.36 us: on_device(): (numerator + anchor * coarse_centroids.astype(F32)) / (denominator[:, Non...]
    unnamed x4 -> x1, local copies, waits for them, and re-layouts: 0.01 us -> 4.79 us
    dot_general x2 -> x0, matrix products: 3.89 us -> none  [the longest x1 2.59 us: on_device(): numerator = lax.dot_general(share, fine_low, TN, preferred_element_type=F32)]
    convert_element_type x0 -> x1, other arithmetic: none -> 2.79 us  [on_device(): return (fine_update, coarse_update.astype(F32))]
    reduce_sum x3 -> x0, other arithmetic: 2.78 us -> none  [the longest x1 1.5 us: on_device(): coarse_sq = jnp.sum(jnp.square(coarse_centroids.astype(F32)), axis=1)]
  transfers between devices with their start and end apart: 1 -> 0, of which waited for: 1 -> 0; matrix products, arithmetic and copies ran while one was open for 0% -> 0% of each run, Pallas kernels for 0% -> 0%
where the time goes in v2:
time: 110 us; the launch traced here: 109 us
  Pallas kernels  101 us (92%)
  local copies, waits for them, and re-layouts  4.79 us (4%)
  other arithmetic  2.79 us (3%)
    pallas_call x1, Pallas kernels, gathered_moments(): pl.pallas_call(functools.partial(gather_kernel, groups, inner, number ==...  101 us
    unnamed x1, local copies, waits for them, and re-layouts  4.79 us
    convert_element_type x1, other arithmetic, on_device(): return (fine_update, coarse_update.astype(F32))  2.79 us

profile of v2, /device:TPU:1, one launch (start us, length us, event | category | flops | bytes accessed | tf_op | source)
XLA Modules:
  0.0 109.4 jit_solution(17447239910012851003)
XLA Ops:
  0.6 101.2 %shard_map.50 = (f32[1024,1024]{1,0:T(8,128)}, f32[1024,128]{1,0:T(8,128)}, bf16[512,1024]{1,0:T(8,128)(2,1)}) custom-call(bf16[128,1024]{1,0:T(8,128)(2,1)} %refs_0_.1, bf16[1024,1024]{1,0:T(8,128)(2,1)} %refs_1_.1, bf16[512,1024]{1,0:T(8,128)(2,1)} %refs_2_.1), custom_call_target="tpu_custom_call" | custom-call | flops 17179869184 | bytes 8388608 | tf_op jit(solution)/shard_map/pallas_call | solution.py:487
  101.9 2.8 %convert_element_type.3 = f32[512,1024]{1,0:T(8,128)} convert(bf16[512,1024]{1,0:T(8,128)(2,1)} %get-tuple-element.5) | non-fusion elementwise | flops 524288 | bytes 3145728 | tf_op jit(solution)/shard_map/convert_element_type | solution.py:512
  104.6 4.8 %copy.6 = f32[1024,1024]{1,0:T(8,128)} copy(f32[1024,1024]{1,0:T(8,128)} %get-tuple-element.8) | data formatting | bytes 8388608

commit v3 on v2

--- a/solution.py
+++ b/solution.py
@@ -38,8 +38,8 @@
     del refs[:2]
     if last_round:
         coarse_out = refs.pop(0)
-    (rows, prob, half_sq, mass, peak, stat,
-     up_send, down_send, z_recv, ring_send, ring_recv, sib_send, sib_recv, stat_send, stat_recv) = refs[:15]
+    (rows, prob, moment, half_sq, mass, peak, stat,
+     up_send, down_send, z_recv, ring_send, ring_recv, sib_send, sib_recv, stat_send, stat_recv, out_sem) = refs[:17]
     layers = inner // 2
     reach = groups // 2
     count = e_ref.shape[0]
@@ -49,6 +49,7 @@
     kl = fine_ref.shape[0]
     kt = tile_of(kl)
     nt = tile_of(width)
+    st = tile_of(kl, 512)
     g = lax.axis_index("grp")
     i = lax.axis_index("inner")
     z = i // 2
@@ -155,16 +156,22 @@
         zz = layer_at(q)
         for slot in slots_of(h):
             sib_arrival(zz, slot).wait_recv()
+        for slot in slots_of(h):
             block = rows[zz, slot].reshape(both, width)
-
-            s = lax.dot_general(fine_ref[...], block, NT, preferred_element_type=F32)
-            s = s * (1.0 / temper) - half_sq[...]
-            top = jnp.max(s, axis=0, keepdims=True)
-            e = jnp.exp(s - top)
-            prob[zz, slot] = e.astype(BF16)
-            total = jnp.sum(e, axis=0, keepdims=True)
-            peak[zz, slot] = top
-            stat[zz, i, slot] = top + jnp.log(total)
+            tops, totals = [], []
+            for t in range(kl // st):
+                ks = pl.ds(t * st, st)
+                s = lax.dot_general(fine_ref[ks, :], block, NT, preferred_element_type=F32)
+                s = s * (1.0 / temper) - half_sq[ks, :]
+                top = jnp.max(s, axis=0, keepdims=True)
+                e = jnp.exp(s - top)
+                prob[zz, slot, ks, :] = e.astype(BF16)
+                peak[zz, slot, t] = top
+                tops.append(top)
+                totals.append(jnp.sum(e, axis=0, keepdims=True))
+            most = functools.reduce(jnp.maximum, tops)
+            total = sum(a * jnp.exp(top - most) for a, top in zip(totals, tops))
+            stat[zz, i, slot] = most + jnp.log(total)
         for off in range(1, inner):
             stat_copy(zz, h, (i + off) % inner).start()
 
@@ -176,30 +183,23 @@
                 lse = stat[zz, :, slot]
                 most = jnp.max(lse, axis=0)
                 lse = most + jnp.log(jnp.sum(jnp.exp(lse - most[None]), axis=0))
-                items.append((zz, slot, jnp.exp(peak[zz, slot] - lse)))
-
-        def scaled(t, carry):
-            ks = pl.ds(pl.multiple_of(t * kt, kt), kt)
+                items.append((zz, slot, lse))
+
+        for t in range(kl // st):
+            ks = pl.ds(t * st, st)
             seen = mass[ks, :]
-            for zz, slot, scale in items:
-                resp = prob[zz, slot, ks, :].astype(F32) * scale
+            parts = []
+            for zz, slot, lse in items:
+                resp = prob[zz, slot, ks, :].astype(F32) * jnp.exp(peak[zz, slot, t] - lse)
                 seen = seen + resp
-                prob[zz, slot, ks, :] = resp.astype(BF16)
+                parts.append(resp.astype(BF16))
             mass[ks, :] = seen
-            return carry
-
-        lax.fori_loop(0, kl // kt, scaled, 0)
-
-        def step(t, carry):
-            ds = pl.ds(pl.multiple_of(t * nt, nt), nt)
-            acc = moment_ref[:, ds]
-            for zz, slot, scale in items:
-                acc = acc + jnp.dot(
-                    prob[zz, slot], rows[zz, slot, :, :, ds].reshape(both, nt), preferred_element_type=F32)
-            moment_ref[:, ds] = acc
-            return carry
-
-        lax.fori_loop(0, width // nt, step, 0)
+            left = jnp.concatenate(parts, axis=1)
+            for d in range(0, width, nt):
+                ds = pl.ds(d, nt)
+                right = jnp.concatenate(
+                    [rows[zz, slot, :, :, ds].reshape(both, nt) for zz, slot, _ in items], axis=0)
+                moment[ks, ds] += jnp.dot(left, right, preferred_element_type=F32)
 
     rows[z, 0, core] = e_ref[...]
     forward(0, 0)
@@ -211,7 +211,7 @@
             (0.5 / temper) * jnp.sum(f * f, axis=1, keepdims=True), (kt, both))
         mass[ks, :] = jnp.zeros((kt, both), F32)
         if not first_round:
-            moment_ref[ks, :] = moment_in[ks, :]
+            moment[ks, :] = moment_in[ks, :]
         return carry
 
     lax.fori_loop(0, kl // kt, squares, 0)
@@ -226,7 +226,7 @@
             logits = logits * (1.0 / temper) - c_half
             e = jnp.exp(logits - jnp.max(logits, axis=1, keepdims=True))
             parent = (e / jnp.sum(e, axis=1, keepdims=True)).astype(BF16)
-            moment_ref[ks, :] = shrink * jnp.dot(parent, coarse_ref[...], preferred_element_type=F32)
+            moment[ks, :] = shrink * jnp.dot(parent, coarse_ref[...], preferred_element_type=F32)
             return carry
 
         lax.fori_loop(0, kl // kt, prior, 0)
@@ -266,8 +266,10 @@
     if not first_round:
         heavy = heavy + mass_in[...]
     mass_ref[...] = heavy
+    written = pltpu.make_async_copy(moment, moment_ref, out_sem.at[0])
+    written.start()
     if last_round:
-        finish(groups, inner, coarse_ref, moment_ref, mass_ref, coarse_out, *refs[15:])
+        finish(groups, inner, coarse_ref, moment, mass_ref, coarse_out, *refs[17:])
 
     def drain(zz, carry):
         @pl.when(goes_up(zz))
@@ -288,6 +290,7 @@
         return carry
 
     lax.fori_loop(0, layers, drain, 0)
+    written.wait()
 
 
 def shares_of(groups, inner, coarse_rows):
@@ -319,9 +322,7 @@
     def child(t, carry):
         ks = pl.ds(pl.multiple_of(t * kt, kt), kt)
         weight = mass_ref[ks, :] + shrink
-        new = moment_ref[ks, :] / weight[:, 0:1]
-        moment_ref[ks, :] = new
-        low = new.astype(BF16)
+        low = (moment_ref[ks, :] * (1.0 / weight[:, 0:1])).astype(BF16)
         fine_low[ks, :] = low
         logits = lax.dot_general(coarse_ref[...], low, NT, preferred_element_type=F32)
         logits = logits * (1.0 / temper) - c_half
@@ -459,14 +460,15 @@
     scratch = [
         pltpu.VMEM((layers, groups, 2, count, width), BF16),
         pltpu.VMEM((layers, groups, kl, both), BF16),
+        pltpu.VMEM((kl, width), F32),
         pltpu.VMEM((kl, both), F32),
         pltpu.VMEM((kl, both), F32),
-        pltpu.VMEM((layers, groups, 1, both), F32),
+        pltpu.VMEM((layers, groups, kl // tile_of(kl, 512), 1, both), F32),
         pltpu.VMEM((layers, inner, groups, 1, both), F32),
         dma((layers,)), dma((layers,)), dma((layers,)),
         dma((2, layers, reach)), dma((2, layers, reach)),
         dma((layers, groups)), dma((layers, groups)),
-        dma((layers, reach + 1)), dma((layers, reach + 1)),
+        dma((layers, reach + 1)), dma((layers, reach + 1)), dma((1,)),
     ]
     if last:
         piece, owners = shares_of(groups, inner, coarse_rows)
@@ -488,13 +490,35 @@
         functools.partial(gather_kernel, groups, inner, number == 0, last),
         out_shape=out_shape,
         in_specs=[vm] * len(args),
-        out_specs=[vm] * len(out_shape),
+        out_specs=[pl.BlockSpec(memory_space=pl.ANY)] + [vm] * (len(out_shape) - 1),
         scratch_shapes=scratch,
         compiler_params=pltpu.CompilerParams(
             collective_id=number, has_side_effects=True, vmem_limit_bytes=60 * 1024 * 1024),
         cost_estimate=pl.CostEstimate(
             flops=4 * total * kl * width, bytes_accessed=8 * kl * width, transcendentals=total * kl),
     )(*args)
+
+
+def output_kernel(moment_ref, mass_ref, coarse_ref, fine_out, coarse_out):
+    fine_out[...] = moment_ref[...] * (1.0 / (mass_ref[:, 0:1] + shrink))
+    coarse_out[...] = coarse_ref[...].astype(F32)
+
+
+def outputs(moment, mass, coarse):
+    steps = 4
+    kl, width = moment.shape
+    coarse_rows = coarse.shape[0]
+
+    def block(count, columns):
+        return pl.BlockSpec((count // steps, columns), lambda t: (t, 0))
+
+    return pl.pallas_call(
+        output_kernel,
+        grid=(steps,),
+        out_shape=[jax.ShapeDtypeStruct((kl, width), F32), jax.ShapeDtypeStruct((coarse_rows, width), F32)],
+        in_specs=[block(kl, width), block(kl, mass.shape[1]), block(coarse_rows, width)],
+        out_specs=[block(kl, width), block(coarse_rows, width)],
+    )(moment, mass, coarse)
 
 
 def on_device(groups, inner, embeds, fine_centroids, coarse_centroids):
@@ -508,8 +532,7 @@
     for r in range(rounds):
         found = gathered_moments(
             groups, inner, r, rounds, embeds[r * step:(r + 1) * step], fine_centroids, coarse_centroids, found[:2])
-    fine_update, _, coarse_update = found
-    return (fine_update, coarse_update.astype(F32))
+    return tuple(outputs(*found))
 
 
 def solution(mesh):

time: 110 us -> 97.2 us (0.88)
  local copies, waits for them, and re-layouts: 4.79 us -> 0 us
  Pallas kernels: 101 us -> 96.3 us
  other arithmetic: 2.79 us -> 0 us
    pallas_call x1, Pallas kernels: 101 us -> 90.7 us  [gathered_moments(): pl.pallas_call(functools.partial(gather_kernel, groups, inner, number ==...]
    pallas_call x0 -> x1, Pallas kernels: none -> 5.63 us  [outputs(): pl.pallas_call(output_kernel, grid=(steps,), out_shape=[jax.ShapeDtypeStr...]
    unnamed x1 -> x0, local copies, waits for them, and re-layouts: 4.79 us -> none
    convert_element_type x1 -> x0, other arithmetic: 2.79 us -> none  [on_device(): return (fine_update, coarse_update.astype(F32))]
where the time goes in v3:
time: 97.2 us; the launch traced here: 97 us
  Pallas kernels  96.3 us (99%)
    pallas_call x1, Pallas kernels, gathered_moments(): pl.pallas_call(functools.partial(gather_kernel, groups, inner, number ==...  90.7 us
    pallas_call x1, Pallas kernels, outputs(): pl.pallas_call(output_kernel, grid=(steps,), out_shape=[jax.ShapeDtypeStr...  5.63 us

profile of v3, /device:TPU:1, one launch (start us, length us, event | category | flops | bytes accessed | tf_op | source)
XLA Modules:
  0.0 97.0 jit_solution(4988583722241265353)
XLA Ops:
  0.6 90.7 %shard_map.50 = (f32[1024,1024]{1,0:T(8,128)}, f32[1024,128]{1,0:T(8,128)}, bf16[512,1024]{1,0:T(8,128)(2,1)}) custom-call(bf16[128,1024]{1,0:T(8,128)(2,1)} %refs_0_.1, bf16[1024,1024]{1,0:T(8,128)(2,1)} %refs_1_.1, bf16[512,1024]{1,0:T(8,128)(2,1)} %refs_2_.1), custom_call_target="tpu_custom_call" | custom-call | flops 17179869184 | bytes 8388608 | tf_op jit(solution)/shard_map/pallas_call | solution.py:489
  91.3 5.6 %shard_map.51 = (f32[1024,1024]{1,0:T(8,128)}, f32[512,1024]{1,0:T(8,128)}) custom-call(f32[1024,1024]{1,0:T(8,128)} %get-tuple-element.5.moment_ref, f32[1024,128]{1,0:T(8,128)} %get-tuple-element.6.mass_ref, bf16[512,1024]{1,0:T(8,128)(2,1)} %get-tuple-element.7.coarse_ref), custom_call_target="tpu_custom_call" | custom-call | tf_op jit(solution)/shard_map/pallas_call | solution.py:515

commit v4 on v3

--- a/solution.py
+++ b/solution.py
@@ -48,7 +48,7 @@
     width = e_ref.shape[1]
     kl = fine_ref.shape[0]
     kt = tile_of(kl)
-    nt = tile_of(width)
+    nt = tile_of(width, 512)
     st = tile_of(kl, 512)
     g = lax.axis_index("grp")
     i = lax.axis_index("inner")
@@ -79,6 +79,9 @@
         if h == reach:
             return (groups - 1,)
         return (2 * h - 1, 2 * h)
+
+    def scored_at(h):
+        return (0, *slots_of(h)) if h == 1 else slots_of(h)
 
     def up_copy(zz):
         block = rows.at[zz, 0, core]
@@ -141,37 +144,40 @@
             sib_copy(zz, slot).start()
 
     def stat_copy(zz, h, peer):
-        slots = slots_of(h)
+        slots = scored_at(h)
         piece = stat.at[zz, i, pl.ds(slots[0], len(slots))]
         return pltpu.make_async_remote_copy(
             piece, piece, stat_send.at[zz, h], stat_recv.at[zz, h], (g, peer), device_id_type=MESH)
 
     def stat_all(zz, h):
-        slots = slots_of(h)
+        slots = scored_at(h)
         piece = stat.at[zz, pl.ds(0, inner - 1), pl.ds(slots[0], len(slots))]
         return pltpu.make_async_remote_copy(
             piece, piece, stat_send.at[zz, h], stat_recv.at[zz, h], (g, (i + 1) % inner), device_id_type=MESH)
 
     def score(h, q):
         zz = layer_at(q)
-        for slot in slots_of(h):
+        slots = scored_at(h)
+        for slot in slots:
             sib_arrival(zz, slot).wait_recv()
-        for slot in slots_of(h):
-            block = rows[zz, slot].reshape(both, width)
-            tops, totals = [], []
-            for t in range(kl // st):
-                ks = pl.ds(t * st, st)
-                s = lax.dot_general(fine_ref[ks, :], block, NT, preferred_element_type=F32)
-                s = s * (1.0 / temper) - half_sq[ks, :]
-                top = jnp.max(s, axis=0, keepdims=True)
-                e = jnp.exp(s - top)
-                prob[zz, slot, ks, :] = e.astype(BF16)
-                peak[zz, slot, t] = top
-                tops.append(top)
-                totals.append(jnp.sum(e, axis=0, keepdims=True))
-            most = functools.reduce(jnp.maximum, tops)
-            total = sum(a * jnp.exp(top - most) for a, top in zip(totals, tops))
-            stat[zz, i, slot] = most + jnp.log(total)
+        block = rows[zz, slots[0]:slots[-1] + 1].reshape(len(slots) * both, width)
+        tops, totals = [], []
+        for t in range(kl // st):
+            ks = pl.ds(t * st, st)
+            s = lax.dot_general(fine_ref[ks, :], block, NT, preferred_element_type=F32)
+            s = s * (1.0 / temper) - jnp.concatenate([half_sq[ks, :]] * len(slots), axis=1)
+            top = jnp.max(s, axis=0, keepdims=True)
+            e = jnp.exp(s - top)
+            for n, slot in enumerate(slots):
+                prob[zz, slot, ks, :] = e[:, n * both:(n + 1) * both].astype(BF16)
+                peak[zz, slot, t] = top[:, n * both:(n + 1) * both]
+            tops.append(top)
+            totals.append(jnp.sum(e, axis=0, keepdims=True))
+        most = functools.reduce(jnp.maximum, tops)
+        total = sum(a * jnp.exp(top - most) for a, top in zip(totals, tops))
+        lse = most + jnp.log(total)
+        for n, slot in enumerate(slots):
+            stat[zz, i, slot] = lse[:, n * both:(n + 1) * both]
         for off in range(1, inner):
             stat_copy(zz, h, (i + off) % inner).start()
 
@@ -179,7 +185,7 @@
         items = []
         for zz in (layers // 2 - 1 - u, layers // 2 + u):
             stat_all(zz, h).wait_recv()
-            for slot in slots_of(h):
+            for slot in scored_at(h):
                 lse = stat[zz, :, slot]
                 most = jnp.max(lse, axis=0)
                 lse = most + jnp.log(jnp.sum(jnp.exp(lse - most[None]), axis=0))
@@ -246,9 +252,8 @@
 
         for h in (0, 1):
             gated(h, forward_later)
-        for h in (0, 1):
-            gated(h, score)
-        for h in range(reach + 1):
+        gated(1, score)
+        for h in range(1, reach + 1):
             u = t - h - 1 - layers // 2
 
             @pl.when(jnp.logical_and(u >= 0, u < layers // 2))
@@ -286,7 +291,8 @@
                     ring_copy(zz, h + 1, way).wait_send()
             for slot in slots_of(h):
                 sib_copy(zz, slot).wait_send()
-            stat_all(zz, h).wait_send()
+            if h > 0:
+                stat_all(zz, h).wait_send()
         return carry
 
     lax.fori_loop(0, layers, drain, 0)
@@ -309,7 +315,7 @@
     coarse_rows = coarse_ref.shape[0]
     piece, owners = shares_of(groups, inner, coarse_rows)
     own_rows = 2 * owners * piece
-    kt = tile_of(kl)
+    kt = tile_of(kl, 512)
     g = lax.axis_index("grp")
     i = lax.axis_index("inner")
     z = i // 2
@@ -505,7 +511,7 @@
 
 
 def outputs(moment, mass, coarse):
-    steps = 4
+    steps = 8
     kl, width = moment.shape
     coarse_rows = coarse.shape[0]
 

time: 97.2 us -> 98.5 us (1.013)
  Pallas kernels: 96.3 us -> 97.6 us
    pallas_call x1, Pallas kernels: 5.63 us -> 7.5 us  [outputs(): pl.pallas_call(output_kernel, grid=(steps,), out_shape=[jax.ShapeDtypeStr...]
where the time goes in v4:
time: 98.5 us; the launch traced here: 98.2 us
  Pallas kernels  97.6 us (99%)
    pallas_call x1, Pallas kernels, gathered_moments(): pl.pallas_call(functools.partial(gather_kernel, groups, inner, number ==...  90.1 us
    pallas_call x1, Pallas kernels, outputs(): pl.pallas_call(output_kernel, grid=(steps,), out_shape=[jax.ShapeDtypeStr...  7.5 us

profile of v4, /device:TPU:1, one launch (start us, length us, event | category | flops | bytes accessed | tf_op | source)
XLA Modules:
  0.0 98.2 jit_solution(14963503249200412784)
XLA Ops:
  0.6 90.1 %shard_map.50 = (f32[1024,1024]{1,0:T(8,128)}, f32[1024,128]{1,0:T(8,128)}, bf16[512,1024]{1,0:T(8,128)(2,1)}) custom-call(bf16[128,1024]{1,0:T(8,128)(2,1)} %refs_0_.1, bf16[1024,1024]{1,0:T(8,128)(2,1)} %refs_1_.1, bf16[512,1024]{1,0:T(8,128)(2,1)} %refs_2_.1), custom_call_target="tpu_custom_call" | custom-call | flops 17179869184 | bytes 8388608 | tf_op jit(solution)/shard_map/pallas_call | solution.py:495
  90.7 7.5 %shard_map.51 = (f32[1024,1024]{1,0:T(8,128)}, f32[512,1024]{1,0:T(8,128)}) custom-call(f32[1024,1024]{1,0:T(8,128)} %get-tuple-element.5.moment_ref, f32[1024,128]{1,0:T(8,128)} %get-tuple-element.6.mass_ref, bf16[512,1024]{1,0:T(8,128)(2,1)} %get-tuple-element.7.coarse_ref), custom_call_target="tpu_custom_call" | custom-call | tf_op jit(solution)/shard_map/pallas_call | solution.py:521

commit v5 on v4

--- a/solution.py
+++ b/solution.py
@@ -511,7 +511,7 @@
 
 
 def outputs(moment, mass, coarse):
-    steps = 8
+    steps = 2
     kl, width = moment.shape
     coarse_rows = coarse.shape[0]
 

time: 98.5 us -> 95.6 us (0.971)
  Pallas kernels: 97.6 us -> 94.8 us
    pallas_call x1, Pallas kernels: 7.5 us -> 4.68 us  [outputs(): pl.pallas_call(output_kernel, grid=(steps,), out_shape=[jax.ShapeDtypeStr...]
where the time goes in v5:
time: 95.6 us; the launch traced here: 95.4 us
  Pallas kernels  94.8 us (99%)
    pallas_call x1, Pallas kernels, gathered_moments(): pl.pallas_call(functools.partial(gather_kernel, groups, inner, number ==...  90.1 us
    pallas_call x1, Pallas kernels, outputs(): pl.pallas_call(output_kernel, grid=(steps,), out_shape=[jax.ShapeDtypeStr...  4.68 us

profile of v5, /device:TPU:1, one launch (start us, length us, event | category | flops | bytes accessed | tf_op | source)
XLA Modules:
  0.0 95.4 jit_solution(8458817212377600082)
XLA Ops:
  0.6 90.1 %shard_map.50 = (f32[1024,1024]{1,0:T(8,128)}, f32[1024,128]{1,0:T(8,128)}, bf16[512,1024]{1,0:T(8,128)(2,1)}) custom-call(bf16[128,1024]{1,0:T(8,128)(2,1)} %refs_0_.1, bf16[1024,1024]{1,0:T(8,128)(2,1)} %refs_1_.1, bf16[512,1024]{1,0:T(8,128)(2,1)} %refs_2_.1), custom_call_target="tpu_custom_call" | custom-call | flops 17179869184 | bytes 8388608 | tf_op jit(solution)/shard_map/pallas_call | solution.py:495
  90.7 4.7 %shard_map.51 = (f32[1024,1024]{1,0:T(8,128)}, f32[512,1024]{1,0:T(8,128)}) custom-call(f32[1024,1024]{1,0:T(8,128)} %get-tuple-element.5.moment_ref, f32[1024,128]{1,0:T(8,128)} %get-tuple-element.6.mass_ref, bf16[512,1024]{1,0:T(8,128)(2,1)} %get-tuple-element.7.coarse_ref), custom_call_target="tpu_custom_call" | custom-call | tf_op jit(solution)/shard_map/pallas_call | solution.py:521
